TPU v7x, 32 devices: a whole 2x2x4 slice. The times are simulated.
32 devices in a mesh: expert: 16 (over z, x, core), dp: 2 (over y).
Axes of the slice: x: 2, y: 2, z: 4, core: 2. Of those that a mesh axis runs over, the one named last changes fastest.
Arguments:
- tokens: bfloat16 [4096, 2048], P(('expert', 'dp')), may hold values from -6 to 6
- w_router: bfloat16 [2048, 16], replicated, may hold values from -0.125 to 0.125
- w_up: bfloat16 [16, 2048, 7168], P('expert', None, 'dp'), may hold values from -0.125 to 0.125
- w_down: bfloat16 [16, 7168, 2048], P('expert', 'dp'), may hold values from -0.0625 to 0.0625
- norm_gain: float32 [2048], replicated, may hold values from 0.25 to 1.75
- readout: bfloat16 [2048, 128], replicated, may hold values from -0.125 to 0.125
- expert_ids: int32 [4096, 2], P(('expert', 'dp')), may hold values from 0 to 15, all different within a row; in each aligned block of 128 rows (0 to 127, 128 to 255, ...) at most 16 rows name the same one
- substation_ids: int32 [4096], P(('expert', 'dp')), may hold values from 0 to 31
- hour_index: int32 [4096], P(('expert', 'dp')), may hold values from 0 to 7
- target: float32 [256, 128], replicated, may hold values from -24 to 24
Outputs:
- load_table: float32 [256, 128], P(('expert', 'dp'))
- loss_value: float32 [], replicated
- grad_down: bfloat16 [16, 7168, 2048], P('expert', 'dp')
Inputs may be any that keep to these rules, and one draw needn't show every extreme that they name: `expert_ids`: each row names two different experts; among the 128 rows of one device every expert is named exactly 16 times.
All inputs are finite; a program needn't handle non-finite values.
Results may differ from a plain program's by a relative error of at most 0.0075.
Values may be sent and summed in bfloat16 or wider, within the bound.
A program may use at most 128 MiB of HBM per device.

v0:
```python
import jax
import jax.numpy as jnp
from jax import lax
from jax.sharding import PartitionSpec as P

HOURS = 8


def local(
    tokens,
    w_router,
    w_up,
    w_down,
    norm_gain,
    readout,
    expert_ids,
    substation_ids,
    hour_index,
    target,
):
    n_expert = lax.axis_size("expert")
    n_group = lax.axis_size("dp")
    tok_rows = tokens.shape[0]
    width = tokens.shape[1]
    capacity = 2 * tok_rows // n_expert
    slots_all = n_expert * capacity
    up_local = w_up[0]
    down_local = w_down[0]
    flat_expert = expert_ids.reshape(-1)
    one_hot = (flat_expert[:, None] == jnp.arange(n_expert, dtype=jnp.int32)[None, :]).astype(
        jnp.int32
    )
    position = jnp.sum((jnp.cumsum(one_hot, axis=0) - 1) * one_hot, axis=1)
    slot_index = flat_expert * capacity + position
    slot_hot = (slot_index[:, None] == jnp.arange(slots_all, dtype=jnp.int32)[None, :]).astype(
        jnp.float32
    )
    slot_pairs = slot_hot.reshape(tok_rows, 2, slots_all)
    placing = jnp.sum(slot_pairs, axis=1).astype(jnp.bfloat16)
    outgoing = lax.dot_general(
        placing, tokens, (((0,), (0,)), ((), ())), preferred_element_type=jnp.float32
    )
    outgoing = outgoing.astype(jnp.bfloat16).reshape(n_expert, capacity, width)
    logits = jnp.dot(tokens, w_router, preferred_element_type=jnp.float32)
    expert_hot = one_hot.reshape(tok_rows, 2, n_expert).astype(jnp.float32)
    chosen = jnp.sum(expert_hot * logits[:, None, :], axis=2)
    gate_first = jax.nn.sigmoid(chosen[:, 0] - chosen[:, 1])
    gate_weights = jnp.stack([gate_first, 1.0 - gate_first], axis=1)
    mixing = jnp.sum(gate_weights[:, :, None] * slot_pairs, axis=1)
    arrived = lax.all_to_all(outgoing, "expert", split_axis=0, concat_axis=0, tiled=True).reshape(
        slots_all, width
    )
    hidden = jax.nn.gelu(
        jnp.dot(
            lax.all_gather(arrived, "dp", axis=0, tiled=True),
            up_local,
            preferred_element_type=jnp.float32,
        )
    ).astype(jnp.bfloat16)
    expert_sum = lax.psum_scatter(
        jnp.dot(hidden, down_local, preferred_element_type=jnp.float32).astype(jnp.bfloat16),
        "dp",
        scatter_dimension=0,
        tiled=True,
    )
    returned = lax.all_to_all(
        expert_sum.reshape(n_expert, capacity, width),
        "expert",
        split_axis=0,
        concat_axis=0,
        tiled=True,
    )
    returned_rows = returned.reshape(slots_all, width).astype(jnp.float32)
    combined = jnp.dot(mixing, returned_rows, precision=lax.Precision.HIGHEST)
    mixed = tokens.astype(jnp.float32) + combined
    rscale = 1.0 / jnp.sqrt(jnp.mean(mixed * mixed, axis=1, keepdims=True) + 1e-05)
    normed = (mixed * rscale * norm_gain[None, :]).astype(jnp.bfloat16)
    loads = jnp.dot(normed, readout, preferred_element_type=jnp.float32)
    n_owner = n_expert * n_group
    key_rows = target.shape[0] // n_owner
    keys = substation_ids * HOURS + hour_index
    key_hot = (keys[None, :] == jnp.arange(target.shape[0], dtype=jnp.int32)[:, None]).astype(
        jnp.float32
    )
    partial_table = jnp.dot(key_hot, loads, precision=lax.Precision.HIGHEST)
    owner_start = lax.axis_index(("expert", "dp")) * key_rows
    table_own = lax.psum_scatter(partial_table, ("expert", "dp"), scatter_dimension=0, tiled=True)
    diff_own = table_own - lax.dynamic_slice_in_dim(target, owner_start, key_rows, 0)
    diff_all = lax.all_gather(diff_own, ("expert", "dp"), axis=0, tiled=True)
    loss_value = 0.5 * jnp.mean(diff_all * diff_all)
    g_loads = lax.dot_general(
        key_hot, diff_all, (((0,), (0,)), ((), ())), precision=lax.Precision.HIGHEST
    )
    g_loads = g_loads.astype(jnp.bfloat16)
    g_normed = lax.dot_general(
        g_loads, readout, (((1,), (1,)), ((), ())), preferred_element_type=jnp.float32
    )
    scaled = g_normed * norm_gain[None, :]
    g_mixed = rscale * scaled - rscale**3 * mixed * jnp.mean(scaled * mixed, axis=1, keepdims=True)
    g_slots = lax.dot_general(
        mixing, g_mixed, (((0,), (0,)), ((), ())), precision=lax.Precision.HIGHEST
    )
    g_slots = g_slots.astype(jnp.bfloat16).reshape(n_expert, capacity, width)
    g_arrived = lax.all_to_all(g_slots, "expert", split_axis=0, concat_axis=0, tiled=True).reshape(
        slots_all, width
    )
    grad_local = lax.dot_general(
        hidden,
        lax.all_gather(g_arrived, "dp", axis=0, tiled=True),
        (((0,), (0,)), ((), ())),
        preferred_element_type=jnp.float32,
    )
    grad_down = grad_local.astype(jnp.bfloat16)[None, :, :]
    return (table_own, loss_value, grad_down)


def solution(mesh):
    placed = (
        P(("expert", "dp"), None),
        P(),
        P("expert", None, "dp"),
        P("expert", "dp", None),
        P(),
        P(),
        P(("expert", "dp"), None),
        P(("expert", "dp")),
        P(("expert", "dp")),
        P(),
    )
    return jax.shard_map(
        local,
        mesh=mesh,
        in_specs=placed,
        out_specs=(P(("expert", "dp"), None), P(), P("expert", "dp", None)),
        check_vma=False,
    )
```

profile of v0, /device:TPU:25, one launch (start us, length us, event | category | flops | bytes accessed | tf_op | source)
XLA Modules:
  0.0 442.6 jit_solution(12628826836050312765)
XLA Ops:
  7.2 0.0 copy-start
  7.2 0.0 all-gather.3.cloned.1.call-start
  7.2 0.8 copy.37
  8.1 0.1 eq.66
  8.2 0.1 eq.62
  8.3 1.3 fusion.35
  9.6 0.7 multiply_reduce_fusion.3
  10.4 0.6 reduce-window.6
  11.0 0.2 slice_reduce_fusion
  11.2 0.1 fusion.33
  11.3 0.1 reduce_sum.66
  11.4 0.1 copy.40
  11.5 0.7 multiply_add_fusion
  12.2 0.1 convert_reduce_fusion
  12.3 1.5 convolution_convert_fusion.1
  13.8 30.0 %all_to_all.15 = bf16[16,16,2048]{2,1,0:T(8,128)(2,1)} all-to-all(bf16[16,16,2048]{2,1,0:T(8,128)(2,1)S(1)} %bitcast.53), channel_id=1, replica_groups=mesh['expert'=16,'dp'=2] {'expert'}, dimensions={0} | all-to-all | bytes 2097152 | tf_op jit(solution)/shard_map/all_to_all | solution.py:50
  43.9 0.0 all-gather.3.cloned.1.call-update
  43.9 0.0 reduce-scatter.2.cloned.1.call-start
  44.0 33.9 %all-gather.3.cloned.1.call-done = bf16[512,2048]{1,0:T(8,128)(2,1)} async-done(((bf16[256,2048]{1,0:T(8,128)(2,1)}), bf16[512,2048]{1,0:T(8,128)(2,1)}) %all-gather.3.cloned.1.call-update) | async-done | bytes 2097168 | tf_op jit(solution)/shard_map/all_gather | solution.py:55
  77.9 12.6 %fusion.12 = bf16[512,3584]{1,0:T(8,128)(2,1)S(1)} fusion(bf16[512,2048]{1,0:T(8,128)(2,1)} %all-gather.3.cloned.1.call-done, bf16[1,2048,3584]{2,1,0:T(8,128)(2,1)} %param.12), kind=kOutput, calls=%fused_computation.14 | convolution fusion | flops 7532707840 | bytes 20447232 | tf_op jit(solution)/shard_map/dot_general | solution.py:54
  90.5 0.0 copy-start.5
  90.5 1.8 copy-done.5
  92.3 12.3 %fusion.15 = bf16[512,2048]{1,0:T(8,128)(2,1)} fusion(bf16[512,3584]{1,0:T(8,128)(2,1)S(1)} %fusion.12, bf16[1,3584,2048]{2,1,0:T(8,128)(2,1)} %param.13), kind=kOutput, calls=%fused_computation.15 | convolution fusion | flops 7517241344 | bytes 20447232 | tf_op jit(solution)/shard_map/dot_general | solution.py:61
  104.6 0.0 reduce-scatter.2.cloned.1.call-update
  104.7 32.0 %reduce-scatter.2.cloned.1.call-done = bf16[256,2048]{1,0:T(8,128)(2,1)} async-done(((bf16[512,2048]{1,0:T(8,128)(2,1)}), bf16[256,2048]{1,0:T(8,128)(2,1)}) %reduce-scatter.2.cloned.1.call-update) | async-done | bytes 1048592 | tf_op jit(solution)/shard_map/reduce_scatter | solution.py:60
  136.6 6.3 %all-to-all-start.1 = ((bf16[16,16,2048]{2,1,0:T(8,128)(2,1)}), bf16[16,16,2048]{2,1,0:T(8,128)(2,1)S(1)}, u32[]{:S(2)}, u32[]{:S(2)}) async-start(bf16[16,16,2048]{2,1,0:T(8,128)(2,1)} %bitcast.54), calls=%async_computation.2 | async-start | bytes 2097152 | tf_op jit(solution)/shard_map/all_to_all | solution.py:66
  143.0 0.0 all-reduce.3.cloned.1.call-start
  143.0 0.0 copy-done.3
  143.0 0.0 copy-done.4
  143.0 22.9 %all-to-all-done.1 = bf16[16,16,2048]{2,1,0:T(8,128)(2,1)S(1)} async-done(((bf16[16,16,2048]{2,1,0:T(8,128)(2,1)}), bf16[16,16,2048]{2,1,0:T(8,128)(2,1)S(1)}, u32[]{:S(2)}, u32[]{:S(2)}) %all-to-all-start.1) | async-done | bytes 1048608 | tf_op jit(solution)/shard_map/all_to_all | solution.py:66
  166.0 0.0 copy-done.1
  166.0 0.8 multiply_reduce_fusion.1
  166.8 0.0 copy-done
  166.8 0.4 fusion.22
  167.2 0.9 fusion.28
  168.1 0.0 all-reduce.3.cloned.1.call-update
  168.1 0.0 all-gather.5.cloned.1.call-start
  168.1 120.4 %all-reduce.3.cloned.1.call-done = f32[256,128]{1,0:T(8,128)} async-done(((f32[256,128]{1,0:T(8,128)}), f32[256,128]{1,0:T(8,128)}) %all-reduce.3.cloned.1.call-update) | async-done | bytes 131088
  288.5 1.3 dynamic-slice_subtract_fusion
  289.8 56.2 %all_gather.10 = f32[256,128]{1,0:T(8,128)S(1)} all-gather(f32[8,128]{1,0:T(8,128)S(1)} %get-tuple-element.5), channel_id=1, replica_groups=mesh['expert'=16,'dp'=2] {'expert','dp'}, dimensions={0}, use_global_device_ids=true | all-gather | bytes 135168 | tf_op jit(solution)/shard_map/all_gather | solution.py:89
  346.0 0.3 convolution_convert_fusion.3
  346.3 0.4 multiply_reduce_fusion
  346.7 2.0 convolution_convert_fusion.2
  348.7 40.1 %all_to_all.16 = bf16[16,16,2048]{2,1,0:T(8,128)(2,1)} all-to-all(bf16[16,16,2048]{2,1,0:T(8,128)(2,1)S(1)} %bitcast.52), channel_id=1, replica_groups=mesh['expert'=16,'dp'=2] {'expert'}, dimensions={0} | all-to-all | bytes 2097152 | tf_op jit(solution)/shard_map/all_to_all | solution.py:104
  388.7 0.0 all-gather.5.cloned.1.call-update
  388.8 0.6 multiply_reduce_fusion.2
  390.0 31.7 %all-gather.5.cloned.1.call-done = bf16[512,2048]{1,0:T(8,128)(2,1)} async-done(((bf16[256,2048]{1,0:T(8,128)(2,1)}), bf16[512,2048]{1,0:T(8,128)(2,1)}) %all-gather.5.cloned.1.call-update) | async-done | bytes 2097168 | tf_op jit(solution)/shard_map/all_gather | solution.py:109
  421.7 13.2 %fusion.4 = bf16[1,3584,2048]{2,1,0:T(8,128)(2,1)} fusion(bf16[512,3584]{1,0:T(8,128)(2,1)} %copy-done.5, bf16[512,2048]{1,0:T(8,128)(2,1)} %all-gather.5.cloned.1.call-done), kind=kOutput, calls=%fused_computation.5 | convolution fusion | flops 7523532800 | bytes 20447232 | tf_op jit(solution)/shard_map/dot_general | solution.py:107
  (13 shorter events, 0.1 us)
Async XLA Ops:
  7.2 159.6 %copy-start = (bf16[2048,128]{1,0:T(8,128)(2,1)S(1)}, bf16[2048,128]{1,0:T(8,128)(2,1)}, u32[]{:S(2)}) copy-start(bf16[2048,128]{1,0:T(8,128)(2,1)} %param.15) | copy-start | bytes 1572868
  7.2 70.7 %all-gather.3.cloned.1.call-start = ((), (), s32[]{:S(2)}) async-start(), calls=%async_computation.4 | async-start | bytes 3145728 | tf_op jit(solution)/shard_map/all_gather | solution.py:55
  43.9 92.7 %reduce-scatter.2.cloned.1.call-start = ((), (), s32[]{:S(2)}) async-start(), calls=%async_computation.5 | async-start | bytes 3145728 | tf_op jit(solution)/shard_map/reduce_scatter | solution.py:60
  90.5 1.8 copy-start.5
  92.3 50.7 %copy-start.3 = (s32[128]{0:T(128)S(1)}, s32[128]{0:T(128)}, u32[]{:S(2)}) copy-start(s32[128]{0:T(128)} %param.18) | copy-start | bytes 1540
  92.3 50.7 %copy-start.4 = (s32[128]{0:T(128)S(1)}, s32[128]{0:T(128)}, u32[]{:S(2)}) copy-start(s32[128]{0:T(128)} %param.17) | copy-start | bytes 1540
  92.3 73.7 %copy-start.1 = (bf16[128,2048]{1,0:T(8,128)(2,1)S(1)}, bf16[128,2048]{1,0:T(8,128)(2,1)}, u32[]{:S(2)}) copy-start(bf16[128,2048]{1,0:T(8,128)(2,1)} %param.10) | copy-start | bytes 1572868
  92.3 74.5 %copy-start.2 = (f32[2048]{0:T(1024)S(1)}, f32[2048]{0:T(1024)}, u32[]{:S(2)}) copy-start(f32[2048]{0:T(1024)} %param.14) | copy-start | bytes 24580
  136.6 29.3 %all-to-all-start.1 = ((bf16[16,16,2048]{2,1,0:T(8,128)(2,1)}), bf16[16,16,2048]{2,1,0:T(8,128)(2,1)S(1)}, u32[]{:S(2)}, u32[]{:S(2)}) async-start(bf16[16,16,2048]{2,1,0:T(8,128)(2,1)} %bitcast.54), calls=%async_computation.2 | async-start | bytes 2097152 | tf_op jit(solution)/shard_map/all_to_all | solution.py:66
  143.0 145.6 %all-reduce.3.cloned.1.call-start = ((), (), s32[]{:S(2)}) async-start(), calls=%async_computation.7 | async-start | bytes 262144
  168.1 253.6 %all-gather.5.cloned.1.call-start = ((), (), s32[]{:S(2)}) async-start(), calls=%async_computation.6 | async-start | bytes 3145728 | tf_op jit(solution)/shard_map/all_gather | solution.py:109
Sparse Core Ops, SparseCore 0:
  44.0 33.7 all-gather.2
  104.8 31.8 reduce-scatter.1
  168.2 120.2 all-reduce.2
  388.9 32.7 all-gather.4
where the time goes:
time: 445 us; the launch traced here: 443 us
  waiting for transfers between devices  241 us (54%)
  blocking collectives  126 us (28%)
  matrix products  45.7 us (10%)
  between operations  15.7 us (4%)
  starting transfers between devices  6.49 us (1%)
    unnamed x5, waiting for transfers between devices  120 us
    all_gather x1, blocking collectives, local(): diff_all = lax.all_gather(diff_own, ('expert', 'dp'), axis=0, tiled=True)  56.2 us
    all_to_all x1, blocking collectives, local(): lax.all_to_all(g_slots, 'expert', split_axis=0, concat_axis=0, tiled=True)  40.1 us
    all_gather x1, waiting for transfers between devices, local(): lax.all_gather(arrived, 'dp', axis=0, tiled=True)  33.9 us
    reduce_scatter x1, waiting for transfers between devices, local(): lax.psum_scatter(jnp.dot(hidden, down_local, preferred_element_type=jnp.f...  32 us
    all_gather x1, waiting for transfers between devices, local(): lax.all_gather(g_arrived, 'dp', axis=0, tiled=True)  31.7 us
    all_to_all x1, blocking collectives, local(): lax.all_to_all(outgoing, 'expert', split_axis=0, concat_axis=0, tiled=True)  30 us
    all_to_all x1, waiting for transfers between devices, local(): lax.all_to_all(expert_sum.reshape(n_expert, capacity, width), 'expert', s...  22.9 us
  transfers between devices with their start and end apart: 5, of which 5 were waited for; matrix products, arithmetic and copies ran while one was open for 0% of the time, Pallas kernels for 0%

commit v1 on v0

--- a/solution.py
+++ b/solution.py
@@ -1,9 +1,268 @@
 import jax
 import jax.numpy as jnp
 from jax import lax
+from jax.experimental import pallas as pl
+from jax.experimental.pallas import tpu as pltpu
 from jax.sharding import PartitionSpec as P
 
 HOURS = 8
+MESH = pl.DeviceIdType.MESH
+
+
+def greet(n_expert, n_group):
+    e, d = lax.axis_index("expert"), lax.axis_index("dp")
+    barrier = pltpu.get_barrier_semaphore()
+
+    @pl.loop(1, n_expert)
+    def _(k):
+        pl.semaphore_signal(
+            barrier, inc=1, device_id=(lax.rem(e + k, n_expert), d), device_id_type=MESH
+        )
+
+    @pl.loop(1, n_group)
+    def _(k):
+        pl.semaphore_signal(
+            barrier, inc=1, device_id=(e, lax.rem(d + k, n_group)), device_id_type=MESH
+        )
+
+    pl.semaphore_wait(barrier, n_expert + n_group - 2)
+
+
+def dispatch_kernel(n_expert, n_group, src, out, own_sem, send_a, recv_a, send_b, recv_b):
+    e, d = lax.axis_index("expert"), lax.axis_index("dp")
+    greet(n_expert, n_group)
+
+    def across(peer, row):
+        return pltpu.make_async_remote_copy(
+            src_ref=src.at[peer],
+            dst_ref=out.at[d, row],
+            send_sem=send_a.at[peer],
+            recv_sem=recv_a.at[row],
+            device_id=(peer, d),
+            device_id_type=MESH,
+        )
+
+    def over(block, row, k):
+        return pltpu.make_async_remote_copy(
+            src_ref=block,
+            dst_ref=out.at[d, row],
+            send_sem=send_b.at[k, row],
+            recv_sem=recv_b.at[k, row],
+            device_id=(e, lax.rem(d + k, n_group)),
+            device_id_type=MESH,
+        )
+
+    @pl.loop(1, n_expert)
+    def _(k):
+        across(lax.rem(e + k, n_expert), e).start()
+
+    own = pltpu.make_async_copy(src.at[e], out.at[d, e], own_sem)
+    own.start()
+    for k in range(1, n_group):
+        over(src.at[e], e, k).start()
+
+    @pl.loop(1, n_expert)
+    def _(k):
+        row = lax.rem(e + n_expert - k, n_expert)
+        across(row, row).wait_recv()
+        for j in range(1, n_group):
+            over(out.at[d, row], row, j).start()
+
+    @pl.loop(0, n_expert)
+    def _(k):
+        row = lax.rem(e + n_expert - k, n_expert)
+        for j in range(1, n_group):
+            over(out.at[d, row], row, j).wait_send()
+            came = lax.rem(d + n_group - j, n_group)
+            pltpu.make_async_remote_copy(
+                src_ref=out.at[came, row],
+                dst_ref=out.at[came, row],
+                send_sem=send_b.at[j, row],
+                recv_sem=recv_b.at[j, row],
+                device_id=(e, came),
+                device_id_type=MESH,
+            ).wait_recv()
+
+    @pl.loop(1, n_expert)
+    def _(k):
+        across(lax.rem(e + k, n_expert), e).wait_send()
+
+    own.wait()
+
+
+def dispatch(blocks, n_group, collective_id):
+    n_expert, capacity, width = blocks.shape
+    return pl.pallas_call(
+        lambda *refs: dispatch_kernel(n_expert, n_group, *refs),
+        out_shape=jax.ShapeDtypeStruct((n_group, n_expert, capacity, width), blocks.dtype),
+        in_specs=[pl.BlockSpec(memory_space=pl.ANY)],
+        out_specs=pl.BlockSpec(memory_space=pl.ANY),
+        scratch_shapes=[
+            pltpu.SemaphoreType.DMA,
+            pltpu.SemaphoreType.DMA((n_expert,)),
+            pltpu.SemaphoreType.DMA((n_expert,)),
+            pltpu.SemaphoreType.DMA((n_group, n_expert)),
+            pltpu.SemaphoreType.DMA((n_group, n_expert)),
+        ],
+        compiler_params=pltpu.CompilerParams(collective_id=collective_id, has_side_effects=True),
+        name="dispatch",
+    )(blocks)
+
+
+def collect_kernel(n_expert, n_group, part, out, held, summed, send_a, recv_a, send_b, recv_b):
+    e, d = lax.axis_index("expert"), lax.axis_index("dp")
+    greet(n_expert, n_group)
+
+    def over(row, j):
+        to = lax.rem(d + j, n_group)
+        return pltpu.make_async_remote_copy(
+            src_ref=part.at[to, row],
+            dst_ref=held.at[j - 1, row],
+            send_sem=send_b.at[j, row],
+            recv_sem=recv_b.at[j, row],
+            device_id=(e, to),
+            device_id_type=MESH,
+        )
+
+    def across(peer, row):
+        return pltpu.make_async_remote_copy(
+            src_ref=summed.at[peer],
+            dst_ref=out.at[row],
+            send_sem=send_a.at[peer],
+            recv_sem=recv_a.at[row],
+            device_id=(peer, d),
+            device_id_type=MESH,
+        )
+
+    def total(row):
+        value = part[d, row].astype(jnp.float32)
+        for j in range(1, n_group):
+            over(row, j).wait_recv()
+            value = value + held[j - 1, row].astype(jnp.float32)
+        return value.astype(out.dtype)
+
+    @pl.loop(1, n_expert + 1)
+    def _(k):
+        row = lax.rem(e + k, n_expert)
+        for j in range(1, n_group):
+            over(row, j).start()
+
+    @pl.loop(1, n_expert)
+    def _(k):
+        row = lax.rem(e + k, n_expert)
+        summed[row] = total(row)
+        across(row, e).start()
+
+    out[e] = total(e)
+
+    @pl.loop(1, n_expert)
+    def _(k):
+        row = lax.rem(e + n_expert - k, n_expert)
+        across(row, row).wait_recv()
+
+    @pl.loop(1, n_expert)
+    def _(k):
+        across(lax.rem(e + k, n_expert), e).wait_send()
+
+    @pl.loop(0, n_expert)
+    def _(row):
+        for j in range(1, n_group):
+            over(row, j).wait_send()
+
+
+def collect(parts, collective_id):
+    n_group, n_expert, capacity, width = parts.shape
+    return pl.pallas_call(
+        lambda *refs: collect_kernel(n_expert, n_group, *refs),
+        out_shape=jax.ShapeDtypeStruct((n_expert, capacity, width), parts.dtype),
+        in_specs=[pl.BlockSpec(memory_space=pltpu.VMEM)],
+        out_specs=pl.BlockSpec(memory_space=pltpu.VMEM),
+        scratch_shapes=[
+            pltpu.VMEM((max(n_group - 1, 1), n_expert, capacity, width), parts.dtype),
+            pltpu.VMEM((n_expert, capacity, width), parts.dtype),
+            pltpu.SemaphoreType.DMA((n_expert,)),
+            pltpu.SemaphoreType.DMA((n_expert,)),
+            pltpu.SemaphoreType.DMA((n_group, n_expert)),
+            pltpu.SemaphoreType.DMA((n_group, n_expert)),
+        ],
+        compiler_params=pltpu.CompilerParams(
+            collective_id=collective_id, has_side_effects=True, vmem_limit_bytes=40 * 2**20
+        ),
+        name="collect",
+    )(parts)
+
+
+def table_kernel(n_expert, n_group, part, target, own, diff, held, send_a, recv_a, send_b, recv_b):
+    n = n_expert * n_group
+    me = lax.axis_index("expert") * n_group + lax.axis_index("dp")
+
+    def place(k):
+        to = lax.rem(me + k, n)
+        return to, (to // n_group, lax.rem(to, n_group))
+
+    barrier = pltpu.get_barrier_semaphore()
+
+    @pl.loop(1, n)
+    def _(k):
+        pl.semaphore_signal(barrier, inc=1, device_id=place(k)[1], device_id_type=MESH)
+
+    pl.semaphore_wait(barrier, n - 1)
+
+    @pl.loop(1, n)
+    def _(k):
+        to, device = place(k)
+        pltpu.make_async_remote_copy(
+            src_ref=part.at[to],
+            dst_ref=held.at[me],
+            send_sem=send_a,
+            recv_sem=recv_a,
+            device_id=device,
+            device_id_type=MESH,
+        ).start()
+
+    held[me] = part[me]
+    rest = pl.ds(0, n - 1)
+    pltpu.make_async_copy(held.at[rest], held.at[rest], recv_a).wait()
+    total = held[0]
+    for i in range(1, n):
+        total = total + held[i]
+    own[...] = total
+    diff[me] = total - target[me]
+
+    @pl.loop(1, n)
+    def _(k):
+        _, device = place(k)
+        pltpu.make_async_remote_copy(
+            src_ref=diff.at[me],
+            dst_ref=diff.at[me],
+            send_sem=send_b,
+            recv_sem=recv_b,
+            device_id=device,
+            device_id_type=MESH,
+        ).start()
+
+    pltpu.make_async_copy(part.at[rest], part.at[rest], send_a).wait()
+    pltpu.make_async_copy(diff.at[rest], diff.at[rest], send_b).wait()
+    pltpu.make_async_copy(diff.at[rest], diff.at[rest], recv_b).wait()
+
+
+def table_sum(part, target, n_expert, n_group, collective_id):
+    n = n_expert * n_group
+    keys, channels = part.shape
+    blocks = (n, keys // n, channels)
+    own, diff = pl.pallas_call(
+        lambda *refs: table_kernel(n_expert, n_group, *refs),
+        out_shape=(
+            jax.ShapeDtypeStruct(blocks[1:], part.dtype),
+            jax.ShapeDtypeStruct(blocks, part.dtype),
+        ),
+        in_specs=[pl.BlockSpec(memory_space=pltpu.VMEM)] * 2,
+        out_specs=[pl.BlockSpec(memory_space=pltpu.VMEM)] * 2,
+        scratch_shapes=[pltpu.VMEM(blocks, part.dtype)] + [pltpu.SemaphoreType.DMA] * 4,
+        compiler_params=pltpu.CompilerParams(collective_id=collective_id, has_side_effects=True),
+        name="table",
+    )(part.reshape(blocks), target.reshape(blocks))
+    return own, diff.reshape(keys, channels)
 
 
 def local(
@@ -30,7 +289,10 @@
     one_hot = (flat_expert[:, None] == jnp.arange(n_expert, dtype=jnp.int32)[None, :]).astype(
         jnp.int32
     )
-    position = jnp.sum((jnp.cumsum(one_hot, axis=0) - 1) * one_hot, axis=1)
+    order = jnp.arange(2 * tok_rows, dtype=jnp.int32)
+    earlier = (order[None, :] < order[:, None]).astype(jnp.bfloat16)
+    before = jnp.dot(earlier, one_hot.astype(jnp.bfloat16), preferred_element_type=jnp.float32)
+    position = jnp.sum(before.astype(jnp.int32) * one_hot, axis=1)
     slot_index = flat_expert * capacity + position
     slot_hot = (slot_index[:, None] == jnp.arange(slots_all, dtype=jnp.int32)[None, :]).astype(
         jnp.float32
@@ -47,46 +309,25 @@
     gate_first = jax.nn.sigmoid(chosen[:, 0] - chosen[:, 1])
     gate_weights = jnp.stack([gate_first, 1.0 - gate_first], axis=1)
     mixing = jnp.sum(gate_weights[:, :, None] * slot_pairs, axis=1)
-    arrived = lax.all_to_all(outgoing, "expert", split_axis=0, concat_axis=0, tiled=True).reshape(
-        slots_all, width
-    )
-    hidden = jax.nn.gelu(
-        jnp.dot(
-            lax.all_gather(arrived, "dp", axis=0, tiled=True),
-            up_local,
-            preferred_element_type=jnp.float32,
-        )
-    ).astype(jnp.bfloat16)
-    expert_sum = lax.psum_scatter(
-        jnp.dot(hidden, down_local, preferred_element_type=jnp.float32).astype(jnp.bfloat16),
-        "dp",
-        scatter_dimension=0,
-        tiled=True,
-    )
-    returned = lax.all_to_all(
-        expert_sum.reshape(n_expert, capacity, width),
-        "expert",
-        split_axis=0,
-        concat_axis=0,
-        tiled=True,
-    )
+    rows_all = n_group * slots_all
+    arrived = dispatch(outgoing, n_group, 1).reshape(rows_all, width)
+    hidden = jax.nn.gelu(jnp.dot(arrived, up_local, preferred_element_type=jnp.float32)).astype(
+        jnp.bfloat16
+    )
+    parts = jnp.dot(hidden, down_local, preferred_element_type=jnp.float32).astype(jnp.bfloat16)
+    returned = collect(parts.reshape(n_group, n_expert, capacity, width), 2)
     returned_rows = returned.reshape(slots_all, width).astype(jnp.float32)
     combined = jnp.dot(mixing, returned_rows, precision=lax.Precision.HIGHEST)
     mixed = tokens.astype(jnp.float32) + combined
     rscale = 1.0 / jnp.sqrt(jnp.mean(mixed * mixed, axis=1, keepdims=True) + 1e-05)
     normed = (mixed * rscale * norm_gain[None, :]).astype(jnp.bfloat16)
     loads = jnp.dot(normed, readout, preferred_element_type=jnp.float32)
-    n_owner = n_expert * n_group
-    key_rows = target.shape[0] // n_owner
     keys = substation_ids * HOURS + hour_index
     key_hot = (keys[None, :] == jnp.arange(target.shape[0], dtype=jnp.int32)[:, None]).astype(
         jnp.float32
     )
     partial_table = jnp.dot(key_hot, loads, precision=lax.Precision.HIGHEST)
-    owner_start = lax.axis_index(("expert", "dp")) * key_rows
-    table_own = lax.psum_scatter(partial_table, ("expert", "dp"), scatter_dimension=0, tiled=True)
-    diff_own = table_own - lax.dynamic_slice_in_dim(target, owner_start, key_rows, 0)
-    diff_all = lax.all_gather(diff_own, ("expert", "dp"), axis=0, tiled=True)
+    table_own, diff_all = table_sum(partial_table, target, n_expert, n_group, 3)
     loss_value = 0.5 * jnp.mean(diff_all * diff_all)
     g_loads = lax.dot_general(
         key_hot, diff_all, (((0,), (0,)), ((), ())), precision=lax.Precision.HIGHEST
@@ -101,12 +342,10 @@
         mixing, g_mixed, (((0,), (0,)), ((), ())), precision=lax.Precision.HIGHEST
     )
     g_slots = g_slots.astype(jnp.bfloat16).reshape(n_expert, capacity, width)
-    g_arrived = lax.all_to_all(g_slots, "expert", split_axis=0, concat_axis=0, tiled=True).reshape(
-        slots_all, width
-    )
+    g_arrived = dispatch(g_slots, n_group, 4).reshape(rows_all, width)
     grad_local = lax.dot_general(
         hidden,
-        lax.all_gather(g_arrived, "dp", axis=0, tiled=True),
+        g_arrived,
         (((0,), (0,)), ((), ())),
         preferred_element_type=jnp.float32,
     )

time: 445 us -> 191 us (0.43)
  waiting for transfers between devices: 241 us -> 0 us
  Pallas kernels: 0 us -> 133 us
  blocking collectives: 126 us -> 0 us
  between operations: 15.7 us -> 2.58 us
  starting transfers between devices: 6.49 us -> 0 us
    pallas_call x0 -> x4, Pallas kernels: none -> 133 us  [the longest x2 82.4 us: dispatch(): pl.pallas_call(lambda *refs: dispatch_kernel(n_expert, n_group, *refs), o...]
    unnamed x5 -> x0, waiting for transfers between devices: 120 us -> none
    all_to_all x2 -> x0, blocking collectives: 70.1 us -> none  [the longest x1 40.1 us: local(): lax.all_to_all(g_slots, 'expert', split_axis=0, concat_axis=0, tiled=True)]
    all_gather x2 -> x0, waiting for transfers between devices: 65.6 us -> none  [the longest x1 33.9 us: local(): lax.all_gather(arrived, 'dp', axis=0, tiled=True)]
    all_gather x1 -> x0, blocking collectives: 56.2 us -> none  [local(): diff_all = lax.all_gather(diff_own, ('expert', 'dp'), axis=0, tiled=True)]
    reduce_scatter x1 -> x0, waiting for transfers between devices: 32 us -> none  [local(): lax.psum_scatter(jnp.dot(hidden, down_local, preferred_element_type=jnp.f...]
    all_to_all x1 -> x0, waiting for transfers between devices: 22.9 us -> none  [local(): lax.all_to_all(expert_sum.reshape(n_expert, capacity, width), 'expert', s...]
    all_to_all x1 -> x0, starting transfers between devices: 6.33 us -> none  [local(): lax.all_to_all(expert_sum.reshape(n_expert, capacity, width), 'expert', s...]
  transfers between devices with their start and end apart: 5 -> 0, of which waited for: 5 -> 0; matrix products, arithmetic and copies ran while one was open for 0% -> 0% of each run, Pallas kernels for 0% -> 0%
where the time goes in v1:
time: 191 us; the launch traced here: 190 us
  Pallas kernels  133 us (70%)
  matrix products  49.2 us (26%)
  other arithmetic  3.88 us (2%)
  between operations  2.58 us (1%)
    pallas_call x2, Pallas kernels, dispatch(): pl.pallas_call(lambda *refs: dispatch_kernel(n_expert, n_group, *refs), o...  82.4 us
    pallas_call x1, Pallas kernels, collect(): pl.pallas_call(lambda *refs: collect_kernel(n_expert, n_group, *refs), ou...  33.2 us
    pallas_call x1, Pallas kernels, table_sum(): pl.pallas_call(lambda *refs: table_kernel(n_expert, n_group, *refs), out_...  17.1 us
    dot_general x1, matrix products, local(): lax.dot_general(hidden, g_arrived, (((0,), (0,)), ((), ())), preferred_el...  13.4 us
    dot_general x1, matrix products, local(): jnp.dot(arrived, up_local, preferred_element_type=jnp.float32)  12.6 us
    dot_general x1, matrix products, local(): jnp.dot(hidden, down_local, preferred_element_type=jnp.float32)  12.6 us

profile of v1, /device:TPU:25, one launch (start us, length us, event | category | flops | bytes accessed | tf_op | source)
XLA Modules:
  0.0 190.1 jit_solution(2963789017882929643)
XLA Ops:
  0.6 0.0 copy-start
  0.6 0.7 multiply_add_fusion.1
  1.4 1.3 fusion.35
  2.7 0.7 multiply_reduce_fusion.3
  3.4 0.8 copy.31
  4.2 0.1 eq.50
  4.3 0.2 fusion.19
  4.5 0.1 reduce_sum.66
  4.7 0.1 copy.32
  4.8 0.7 multiply_add_fusion
  5.5 0.1 convert_reduce_fusion
  5.6 2.5 %convolution_convert_fusion.1 = bf16[256,2048]{1,0:T(8,128)(2,1)} fusion(bf16[128,2048]{1,0:T(8,128)(2,1)} %param.10, bf16[128,256]{1,0:T(8,128)(2,1)S(1)} %get-tuple-element.7), kind=kOutput, calls=%fused_computation.16 | convolution fusion | flops 134742016 | bytes 1638400 | tf_op jit(solution)/shard_map/dot_general | solution.py:302
  8.1 41.8 %dispatch.2 = bf16[2,16,16,2048]{3,2,1,0:T(8,128)(2,1)} custom-call(bf16[16,16,2048]{2,1,0:T(8,128)(2,1)} %bitcast.42), custom_call_target="tpu_custom_call" | custom-call | tf_op jit(solution)/shard_map/dispatch/pallas_call | solution.py:95
  49.9 12.6 %fusion.12 = bf16[512,3584]{1,0:T(8,128)(2,1)S(1)} fusion(bf16[512,2048]{1,0:T(8,128)(2,1)} %bitcast.44, bf16[1,2048,3584]{2,1,0:T(8,128)(2,1)} %param.12), kind=kOutput, calls=%fused_computation.14 | convolution fusion | flops 7532707840 | bytes 20447232 | tf_op jit(solution)/shard_map/dot_general | solution.py:314
  62.6 0.0 copy-start.4
  62.6 0.0 copy-start.1
  62.6 0.0 copy-start.2
  62.6 12.6 %fusion.15 = bf16[512,2048]{1,0:T(8,128)(2,1)S(1)} fusion(bf16[512,3584]{1,0:T(8,128)(2,1)S(1)} %fusion.12, bf16[1,3584,2048]{2,1,0:T(8,128)(2,1)} %param.13), kind=kOutput, calls=%fused_computation.15 | convolution fusion | flops 7517241344 | bytes 20447232 | tf_op jit(solution)/shard_map/dot_general | solution.py:317
  75.2 0.0 copy-done.4
  75.2 33.2 %collect.1 = bf16[16,16,2048]{2,1,0:T(8,128)(2,1)S(1)} custom-call(bf16[2,16,16,2048]{3,2,1,0:T(8,128)(2,1)S(1)} %bitcast.40), custom_call_target="tpu_custom_call" | custom-call | tf_op jit(solution)/shard_map/collect/pallas_call | solution.py:175
  108.4 0.0 copy-done.1
  108.4 0.8 multiply_reduce_fusion.1
  109.2 0.0 copy-done
  109.2 0.0 copy-done.2
  109.2 0.4 fusion.24
  109.6 0.9 convolution_bitcast_fusion.refs_0_
  110.5 17.1 %table.1 = (f32[8,128]{1,0:T(8,128)}, f32[32,8,128]{2,1,0:T(8,128)}) custom-call(f32[32,8,128]{2,1,0:T(8,128)} %convolution_bitcast_fusion.refs_0_, f32[32,8,128]{2,1,0:T(8,128)} %bitcast.45), custom_call_target="tpu_custom_call" | custom-call | tf_op jit(solution)/shard_map/table/pallas_call | solution.py:253
  127.6 1.5 multiply_reduce_fusion.2
  129.8 1.2 convolution_convert_fusion.3
  131.0 0.4 multiply_reduce_fusion
  131.4 3.0 %convolution_convert_fusion.2 = bf16[256,2048]{1,0:T(8,128)(2,1)} fusion(f32[128,256]{1,0:T(8,128)S(1)} %get-tuple-element.8, f32[128,2048]{1,0:T(8,128)S(1)} %get-tuple-element.14, f32[128,2048]{1,0:T(8,128)S(1)} %get-tuple-element.16, f32[128]{0:T(128)S(1)} %broadcast_multiply_fusion, f32[128]{0:T(128)S(1)} %get-tuple-element.11, ...), kind=kOutput, calls=%fused_computation.17 | convolution fusion | flops 806879232 | bytes 3278336 | tf_op jit(solution)/shard_map/dot_general | solution.py:341
  134.4 40.6 %dispatch.3 = bf16[2,16,16,2048]{3,2,1,0:T(8,128)(2,1)} custom-call(bf16[16,16,2048]{2,1,0:T(8,128)(2,1)} %bitcast.41), custom_call_target="tpu_custom_call" | custom-call | tf_op jit(solution)/shard_map/dispatch/pallas_call | solution.py:95
  175.0 0.0 copy-start.3
  175.0 13.4 %fusion.4 = bf16[1,3584,2048]{2,1,0:T(8,128)(2,1)} fusion(bf16[512,3584]{1,0:T(8,128)(2,1)} %copy-done.4, bf16[512,2048]{1,0:T(8,128)(2,1)} %bitcast.43), kind=kOutput, calls=%fused_computation.5 | convolution fusion | flops 7523532800 | bytes 20447232 | tf_op jit(solution)/shard_map/dot_general | solution.py:346
  188.4 0.0 copy-done.3
  188.4 0.6 copy.34
  (4 shorter events, 0.0 us)
Async XLA Ops:
  0.6 108.6 %copy-start = (bf16[2048,128]{1,0:T(8,128)(2,1)S(1)}, bf16[2048,128]{1,0:T(8,128)(2,1)}, u32[]{:S(2)}) copy-start(bf16[2048,128]{1,0:T(8,128)(2,1)} %param.15) | copy-start | bytes 1572868
  62.6 12.7 %copy-start.4 = (bf16[512,3584]{1,0:T(8,128)(2,1)}, bf16[512,3584]{1,0:T(8,128)(2,1)S(1)}, u32[]{:S(2)}) copy-start(bf16[512,3584]{1,0:T(8,128)(2,1)S(1)} %fusion.12) | copy-start | bytes 11010052
  62.6 45.8 %copy-start.1 = (bf16[128,2048]{1,0:T(8,128)(2,1)S(1)}, bf16[128,2048]{1,0:T(8,128)(2,1)}, u32[]{:S(2)}) copy-start(bf16[128,2048]{1,0:T(8,128)(2,1)} %param.10) | copy-start | bytes 1572868
  62.6 46.6 %copy-start.2 = (f32[2048]{0:T(1024)S(1)}, f32[2048]{0:T(1024)}, u32[]{:S(2)}) copy-start(f32[2048]{0:T(1024)} %param.14) | copy-start | bytes 24580
  175.0 13.4 %copy-start.3 = (f32[8,128]{1,0:T(8,128)S(1)}, f32[8,128]{1,0:T(8,128)}, u32[]{:S(2)}) copy-start(f32[8,128]{1,0:T(8,128)} %get-tuple-element.20) | copy-start | bytes 12292

commit v2 on v1

--- a/solution.py
+++ b/solution.py
@@ -28,66 +28,90 @@
     pl.semaphore_wait(barrier, n_expert + n_group - 2)
 
 
-def dispatch_kernel(n_expert, n_group, src, out, own_sem, send_a, recv_a, send_b, recv_b):
-    e, d = lax.axis_index("expert"), lax.axis_index("dp")
-    greet(n_expert, n_group)
-
-    def across(peer, row):
+class Rows:
+    def __init__(self, n_expert, n_group, src, out, own_sem, send_a, recv_a, send_b, recv_b):
+        self.n_expert, self.n_group = n_expert, n_group
+        self.src, self.out = src, out
+        self.send_a, self.recv_a, self.send_b, self.recv_b = send_a, recv_a, send_b, recv_b
+        self.e, self.d = lax.axis_index("expert"), lax.axis_index("dp")
+        self.own = pltpu.make_async_copy(src.at[self.e], out.at[self.d, self.e], own_sem)
+
+    def across(self, peer, row):
         return pltpu.make_async_remote_copy(
-            src_ref=src.at[peer],
-            dst_ref=out.at[d, row],
-            send_sem=send_a.at[peer],
-            recv_sem=recv_a.at[row],
-            device_id=(peer, d),
-            device_id_type=MESH,
-        )
-
-    def over(block, row, k):
+            src_ref=self.src.at[peer],
+            dst_ref=self.out.at[self.d, row],
+            send_sem=self.send_a.at[peer],
+            recv_sem=self.recv_a.at[row],
+            device_id=(peer, self.d),
+            device_id_type=MESH,
+        )
+
+    def over(self, block, row, k):
         return pltpu.make_async_remote_copy(
             src_ref=block,
-            dst_ref=out.at[d, row],
-            send_sem=send_b.at[k, row],
-            recv_sem=recv_b.at[k, row],
-            device_id=(e, lax.rem(d + k, n_group)),
-            device_id_type=MESH,
-        )
-
-    @pl.loop(1, n_expert)
-    def _(k):
-        across(lax.rem(e + k, n_expert), e).start()
-
-    own = pltpu.make_async_copy(src.at[e], out.at[d, e], own_sem)
-    own.start()
-    for k in range(1, n_group):
-        over(src.at[e], e, k).start()
-
-    @pl.loop(1, n_expert)
-    def _(k):
-        row = lax.rem(e + n_expert - k, n_expert)
-        across(row, row).wait_recv()
-        for j in range(1, n_group):
-            over(out.at[d, row], row, j).start()
-
-    @pl.loop(0, n_expert)
-    def _(k):
-        row = lax.rem(e + n_expert - k, n_expert)
-        for j in range(1, n_group):
-            over(out.at[d, row], row, j).wait_send()
-            came = lax.rem(d + n_group - j, n_group)
-            pltpu.make_async_remote_copy(
-                src_ref=out.at[came, row],
-                dst_ref=out.at[came, row],
-                send_sem=send_b.at[j, row],
-                recv_sem=recv_b.at[j, row],
-                device_id=(e, came),
-                device_id_type=MESH,
-            ).wait_recv()
-
-    @pl.loop(1, n_expert)
-    def _(k):
-        across(lax.rem(e + k, n_expert), e).wait_send()
-
-    own.wait()
+            dst_ref=self.out.at[self.d, row],
+            send_sem=self.send_b.at[k, row],
+            recv_sem=self.recv_b.at[k, row],
+            device_id=(self.e, lax.rem(self.d + k, self.n_group)),
+            device_id_type=MESH,
+        )
+
+    def start(self):
+        @pl.loop(1, self.n_expert)
+        def _(k):
+            self.across(lax.rem(self.e + k, self.n_expert), self.e).start()
+
+        self.own.start()
+        for k in range(1, self.n_group):
+            self.over(self.src.at[self.e], self.e, k).start()
+
+    def forward(self, first, last):
+        @pl.loop(first, last)
+        def _(k):
+            row = lax.rem(self.e + self.n_expert - k, self.n_expert)
+            self.across(row, row).wait_recv()
+            for j in range(1, self.n_group):
+                self.over(self.out.at[self.d, row], row, j).start()
+
+    def finish(self):
+        @pl.loop(0, self.n_expert)
+        def _(k):
+            row = lax.rem(self.e + self.n_expert - k, self.n_expert)
+            for j in range(1, self.n_group):
+                self.over(self.out.at[self.d, row], row, j).wait_send()
+                came = lax.rem(self.d + self.n_group - j, self.n_group)
+                pltpu.make_async_remote_copy(
+                    src_ref=self.out.at[came, row],
+                    dst_ref=self.out.at[came, row],
+                    send_sem=self.send_b.at[j, row],
+                    recv_sem=self.recv_b.at[j, row],
+                    device_id=(self.e, came),
+                    device_id_type=MESH,
+                ).wait_recv()
+
+        @pl.loop(1, self.n_expert)
+        def _(k):
+            self.across(lax.rem(self.e + k, self.n_expert), self.e).wait_send()
+
+        self.own.wait()
+
+
+def row_semaphores(n_expert, n_group):
+    return [
+        pltpu.SemaphoreType.DMA,
+        pltpu.SemaphoreType.DMA((n_expert,)),
+        pltpu.SemaphoreType.DMA((n_expert,)),
+        pltpu.SemaphoreType.DMA((n_group, n_expert)),
+        pltpu.SemaphoreType.DMA((n_group, n_expert)),
+    ]
+
+
+def dispatch_kernel(n_expert, n_group, *refs):
+    rows = Rows(n_expert, n_group, *refs)
+    greet(n_expert, n_group)
+    rows.start()
+    rows.forward(1, n_expert)
+    rows.finish()
 
 
 def dispatch(blocks, n_group, collective_id):
@@ -97,13 +121,7 @@
         out_shape=jax.ShapeDtypeStruct((n_group, n_expert, capacity, width), blocks.dtype),
         in_specs=[pl.BlockSpec(memory_space=pl.ANY)],
         out_specs=pl.BlockSpec(memory_space=pl.ANY),
-        scratch_shapes=[
-            pltpu.SemaphoreType.DMA,
-            pltpu.SemaphoreType.DMA((n_expert,)),
-            pltpu.SemaphoreType.DMA((n_expert,)),
-            pltpu.SemaphoreType.DMA((n_group, n_expert)),
-            pltpu.SemaphoreType.DMA((n_group, n_expert)),
-        ],
+        scratch_shapes=row_semaphores(n_expert, n_group),
         compiler_params=pltpu.CompilerParams(collective_id=collective_id, has_side_effects=True),
         name="dispatch",
     )(blocks)
@@ -192,7 +210,23 @@
     )(parts)
 
 
-def table_kernel(n_expert, n_group, part, target, own, diff, held, send_a, recv_a, send_b, recv_b):
+def exchange_kernel(
+    n_expert,
+    n_group,
+    part,
+    target,
+    blocks,
+    own,
+    diff,
+    out,
+    held,
+    send_a,
+    recv_a,
+    send_b,
+    recv_b,
+    *row_sems,
+):
+    rows = Rows(n_expert, n_group, blocks, out, *row_sems)
     n = n_expert * n_group
     me = lax.axis_index("expert") * n_group + lax.axis_index("dp")
 
@@ -220,6 +254,9 @@
             device_id_type=MESH,
         ).start()
 
+    rows.start()
+    early = 1 + n_expert // 4
+    rows.forward(1, early)
     held[me] = part[me]
     rest = pl.ds(0, n - 1)
     pltpu.make_async_copy(held.at[rest], held.at[rest], recv_a).wait()
@@ -241,28 +278,40 @@
             device_id_type=MESH,
         ).start()
 
+    rows.forward(early, n_expert)
+    rows.finish()
     pltpu.make_async_copy(part.at[rest], part.at[rest], send_a).wait()
     pltpu.make_async_copy(diff.at[rest], diff.at[rest], send_b).wait()
     pltpu.make_async_copy(diff.at[rest], diff.at[rest], recv_b).wait()
 
 
-def table_sum(part, target, n_expert, n_group, collective_id):
+def exchange(part, target, rows, n_group, collective_id):
+    n_expert, capacity, width = rows.shape
     n = n_expert * n_group
     keys, channels = part.shape
     blocks = (n, keys // n, channels)
-    own, diff = pl.pallas_call(
-        lambda *refs: table_kernel(n_expert, n_group, *refs),
+    own, diff, out = pl.pallas_call(
+        lambda *refs: exchange_kernel(n_expert, n_group, *refs),
         out_shape=(
             jax.ShapeDtypeStruct(blocks[1:], part.dtype),
             jax.ShapeDtypeStruct(blocks, part.dtype),
+            jax.ShapeDtypeStruct((n_group, n_expert, capacity, width), rows.dtype),
         ),
-        in_specs=[pl.BlockSpec(memory_space=pltpu.VMEM)] * 2,
-        out_specs=[pl.BlockSpec(memory_space=pltpu.VMEM)] * 2,
-        scratch_shapes=[pltpu.VMEM(blocks, part.dtype)] + [pltpu.SemaphoreType.DMA] * 4,
+        in_specs=[pl.BlockSpec(memory_space=pltpu.VMEM)] * 2 + [pl.BlockSpec(memory_space=pl.ANY)],
+        out_specs=[pl.BlockSpec(memory_space=pltpu.VMEM)] * 2
+        + [pl.BlockSpec(memory_space=pl.ANY)],
+        scratch_shapes=[pltpu.VMEM(blocks, part.dtype)]
+        + [pltpu.SemaphoreType.DMA] * 4
+        + row_semaphores(n_expert, n_group),
         compiler_params=pltpu.CompilerParams(collective_id=collective_id, has_side_effects=True),
-        name="table",
-    )(part.reshape(blocks), target.reshape(blocks))
-    return own, diff.reshape(keys, channels)
+        name="exchange",
+    )(part.reshape(blocks), target.reshape(blocks), rows)
+    return own, diff.reshape(keys, channels), out
+
+
+def halves(value):
+    high = lax.reduce_precision(value, 8, 7)
+    return [high.astype(jnp.bfloat16), (value - high).astype(jnp.bfloat16)]
 
 
 def local(
@@ -327,22 +376,43 @@
         jnp.float32
     )
     partial_table = jnp.dot(key_hot, loads, precision=lax.Precision.HIGHEST)
-    table_own, diff_all = table_sum(partial_table, target, n_expert, n_group, 3)
+    slots_of = jnp.sum(slot_pairs, axis=1)
+    scale_slots = jnp.sum(slots_of * rscale, axis=0)
+    gate_slots = jnp.sum(mixing, axis=0)
+    key_slots = jnp.sum(slots_of * keys.astype(jnp.float32)[:, None], axis=0)
+    columns = jnp.stack(
+        halves(gate_slots * scale_slots) + halves(scale_slots * scale_slots) + halves(key_slots),
+        axis=1,
+    )
+    lanes = 128
+    columns = jnp.pad(columns, ((0, 0), (0, lanes - columns.shape[1])))
+    mixed_slots = lax.dot_general(
+        placing,
+        mixed.astype(jnp.bfloat16),
+        (((0,), (0,)), ((), ())),
+        preferred_element_type=jnp.float32,
+    ).astype(jnp.bfloat16)
+    sent = jnp.concatenate([mixed_slots, columns], axis=1)
+    table_own, diff_all, came = exchange(
+        partial_table, target, sent.reshape(n_expert, capacity, width + lanes), n_group, 3
+    )
     loss_value = 0.5 * jnp.mean(diff_all * diff_all)
-    g_loads = lax.dot_general(
-        key_hot, diff_all, (((0,), (0,)), ((), ())), precision=lax.Precision.HIGHEST
-    )
-    g_loads = g_loads.astype(jnp.bfloat16)
+    came = came.reshape(rows_all, width + lanes)
+    mixed_came = came[:, :width].astype(jnp.float32)
+    pairs = came[:, width:].astype(jnp.float32)
+    gate_scale = pairs[:, 0:1] + pairs[:, 1:2]
+    scale_squared = pairs[:, 2:3] + pairs[:, 3:4]
+    key_came = (pairs[:, 4:5] + pairs[:, 5:6]).astype(jnp.int32)
+    came_hot = (key_came == jnp.arange(target.shape[0], dtype=jnp.int32)[None, :]).astype(
+        jnp.float32
+    )
+    g_loads = jnp.dot(came_hot, diff_all, precision=lax.Precision.HIGHEST).astype(jnp.bfloat16)
     g_normed = lax.dot_general(
         g_loads, readout, (((1,), (1,)), ((), ())), preferred_element_type=jnp.float32
     )
     scaled = g_normed * norm_gain[None, :]
-    g_mixed = rscale * scaled - rscale**3 * mixed * jnp.mean(scaled * mixed, axis=1, keepdims=True)
-    g_slots = lax.dot_general(
-        mixing, g_mixed, (((0,), (0,)), ((), ())), precision=lax.Precision.HIGHEST
-    )
-    g_slots = g_slots.astype(jnp.bfloat16).reshape(n_expert, capacity, width)
-    g_arrived = dispatch(g_slots, n_group, 4).reshape(rows_all, width)
+    along = scale_squared * jnp.mean(scaled * mixed_came, axis=1, keepdims=True)
+    g_arrived = (gate_scale * (scaled - mixed_came * along)).astype(jnp.bfloat16)
     grad_local = lax.dot_general(
         hidden,
         g_arrived,

time: 191 us -> 190 us (level)
  Pallas kernels: 133 us -> 126 us
  other arithmetic: 3.88 us -> 6.78 us
  matrix products: 49.2 us -> 52 us
    pallas_call x2 -> x1, Pallas kernels: 82.4 us -> 41.8 us  [dispatch(): pl.pallas_call(lambda *refs: dispatch_kernel(n_expert, n_group, *refs), o...]
    pallas_call x1, Pallas kernels: 17.1 us -> 51 us  [exchange(): pl.pallas_call(lambda *refs: exchange_kernel(n_expert, n_group, *refs), o...]
    dot_general x1, matrix products: 0.38 us -> 4.4 us  [local(): lax.dot_general(g_loads, readout, (((1,), (1,)), ((), ())), preferred_ele...]
    dot_general x2, matrix products: 4.15 us -> 1.78 us  [the longest x1 1.32 us: local(): jnp.dot(came_hot, diff_all, precision=lax.Precision.HIGHEST)]
    convert_element_type x0 -> x5, other arithmetic: none -> 1.97 us  [the longest x1 0.92 us: local(): pairs = came[:, width:].astype(jnp.float32)]
where the time goes in v2:
time: 190 us; the launch traced here: 189 us
  Pallas kernels  126 us (66%)
  matrix products  52 us (27%)
  other arithmetic  6.78 us (4%)
  between operations  2.62 us (1%)
  local copies, waits for them, and re-layouts  2.07 us (1%)
    pallas_call x1, Pallas kernels, exchange(): pl.pallas_call(lambda *refs: exchange_kernel(n_expert, n_group, *refs), o...  51 us
    pallas_call x1, Pallas kernels, dispatch(): pl.pallas_call(lambda *refs: dispatch_kernel(n_expert, n_group, *refs), o...  41.8 us
    pallas_call x1, Pallas kernels, collect(): pl.pallas_call(lambda *refs: collect_kernel(n_expert, n_group, *refs), ou...  33.2 us
    dot_general x1, matrix products, local(): lax.dot_general(hidden, g_arrived, (((0,), (0,)), ((), ())), preferred_el...  14.6 us
    dot_general x1, matrix products, local(): jnp.dot(arrived, up_local, preferred_element_type=jnp.float32)  12.7 us
    dot_general x1, matrix products, local(): jnp.dot(hidden, down_local, preferred_element_type=jnp.float32)  12.6 us
    dot_general x1, matrix products, local(): lax.dot_general(g_loads, readout, (((1,), (1,)), ((), ())), preferred_ele...  4.4 us

profile of v2, /device:TPU:25, one launch (start us, length us, event | category | flops | bytes accessed | tf_op | source)
XLA Modules:
  0.0 189.4 jit_solution(15017315105159348414)
XLA Ops:
  0.6 0.0 copy-start
  0.6 0.7 fusion.49
  1.4 1.3 fusion.51
  2.7 0.7 multiply_reduce_fusion.4
  3.4 0.8 copy.42
  4.2 0.1 eq.65
  4.3 0.2 fusion.30
  4.5 0.1 reduce_sum.99
  4.7 0.1 copy.43
  4.8 0.7 multiply_add_fusion
  5.5 0.1 select_reduce_fusion
  5.6 2.5 %convolution_convert_fusion.2 = bf16[256,2048]{1,0:T(8,128)(2,1)} fusion(bf16[128,2048]{1,0:T(8,128)(2,1)} %param.10, f32[128,256]{1,0:T(8,128)S(1)} %get-tuple-element.15), kind=kOutput, calls=%fused_computation.23 | convolution fusion | flops 134774784 | bytes 1703936 | tf_op jit(solution)/shard_map/dot_general | solution.py:351
  8.1 41.8 %dispatch.1 = bf16[2,16,16,2048]{3,2,1,0:T(8,128)(2,1)} custom-call(bf16[16,16,2048]{2,1,0:T(8,128)(2,1)} %bitcast.43), custom_call_target="tpu_custom_call" | custom-call | tf_op jit(solution)/shard_map/dispatch/pallas_call | solution.py:119
  49.9 12.7 %fusion.12 = bf16[512,3584]{1,0:T(8,128)(2,1)S(1)} fusion(bf16[512,2048]{1,0:T(8,128)(2,1)} %bitcast.47, bf16[1,2048,3584]{2,1,0:T(8,128)(2,1)} %param.12), kind=kOutput, calls=%fused_computation.14 | convolution fusion | flops 7532707840 | bytes 20447232 | tf_op jit(solution)/shard_map/dot_general | solution.py:363
  62.6 0.0 copy-start.5
  62.6 0.0 copy-start.1
  62.6 12.6 %fusion.19 = bf16[512,2048]{1,0:T(8,128)(2,1)S(1)} fusion(bf16[512,3584]{1,0:T(8,128)(2,1)S(1)} %fusion.12, bf16[1,3584,2048]{2,1,0:T(8,128)(2,1)} %param.13), kind=kOutput, calls=%fused_computation.21 | convolution fusion | flops 7517241344 | bytes 20447232 | tf_op jit(solution)/shard_map/dot_general | solution.py:366
  75.2 0.0 copy-done.5
  75.2 0.0 copy-start.3
  75.3 33.2 %collect.1 = bf16[16,16,2048]{2,1,0:T(8,128)(2,1)S(1)} custom-call(bf16[2,16,16,2048]{3,2,1,0:T(8,128)(2,1)S(1)} %bitcast.41), custom_call_target="tpu_custom_call" | custom-call | tf_op jit(solution)/shard_map/collect/pallas_call | solution.py:193
  108.4 0.0 copy-done.1
  108.4 0.8 multiply_reduce_fusion
  109.2 0.1 multiply_reduce_fusion.2
  109.4 0.1 copy.44
  109.5 0.0 copy-done
  109.5 0.0 copy-done.3
  109.6 0.3 fusion.31
  109.9 0.5 convolution_convert_fusion.1
  110.4 1.1 fusion.28
  111.5 0.8 convolution_bitcast_fusion.refs_0_
  112.3 51.0 %exchange.1 = (f32[8,128]{1,0:T(8,128)}, f32[32,8,128]{2,1,0:T(8,128)}, bf16[2,16,16,2176]{3,2,1,0:T(8,128)(2,1)}) custom-call(f32[32,8,128]{2,1,0:T(8,128)} %convolution_bitcast_fusion.refs_0_, f32[32,8,128]{2,1,0:T(8,128)} %bitcast.48, bf16[16,16,2176]{2,1,0:T(8,128)(2,1)} %bitcast.42), custom_call_target="tpu_custom_call" | custom-call | tf_op jit(solution)/shard_map/exchange/pallas_call | solution.py:293
  163.3 1.5 multiply_reduce_fusion.1
  165.5 0.9 slice_convert_fusion
  166.4 0.3 fusion.38
  166.7 1.3 convolution_convert_fusion.3
  168.0 0.0 copy-start.2
  168.0 4.4 %fusion.15 = (f32[512]{0:T(512)S(1)}, f32[512,2048]{1,0:T(8,128)}) fusion(f32[2048]{0:T(1024)S(1)} %copy-done.3, bf16[512,2176]{1,0:T(8,128)(2,1)} %bitcast.45, bf16[512,128]{1,0:T(8,128)(2,1)S(1)} %convolution_convert_fusion.3, bf16[2048,128]{1,0:T(8,128)(2,1)S(1)} %copy-done), kind=kOutput, calls=%fused_computation.17 | convolution fusion | flops 272629248 | bytes 6957056 | tf_op jit(solution)/shard_map/dot_general | solution.py:410
  172.4 0.1 copy.45
  172.6 0.4 fusion.39
  173.0 0.0 copy-done.2
  173.0 0.0 copy-start.4
  173.1 14.6 %fusion.4 = bf16[1,3584,2048]{2,1,0:T(8,128)(2,1)} fusion(bf16[512,3584]{1,0:T(8,128)(2,1)} %copy-done.5, f32[512,2048]{1,0:T(8,128)} %get-tuple-element.31, f32[512]{0:T(512)S(1)} %get-tuple-element.10, f32[2048]{0:T(1024)S(1)} %copy-done.3, f32[512]{0:T(512)S(1)} %get-tuple-element.9, bf16[512,2176]{1,0:T(8,128)(2,1)S(1)} %bitcast.46), kind=kOutput, calls=%fused_computation.5 | convolution fusion | flops 7529824256 | bytes 24653824 | tf_op jit(solution)/shard_map/dot_general | solution.py:416
  187.7 0.0 copy-done.4
  187.7 0.6 copy.47
  (8 shorter events, 0.1 us)
Async XLA Ops:
  0.6 108.9 %copy-start = (bf16[2048,128]{1,0:T(8,128)(2,1)S(1)}, bf16[2048,128]{1,0:T(8,128)(2,1)}, u32[]{:S(2)}) copy-start(bf16[2048,128]{1,0:T(8,128)(2,1)} %param.15) | copy-start | bytes 1572868
  62.6 12.7 %copy-start.5 = (bf16[512,3584]{1,0:T(8,128)(2,1)}, bf16[512,3584]{1,0:T(8,128)(2,1)S(1)}, u32[]{:S(2)}) copy-start(bf16[512,3584]{1,0:T(8,128)(2,1)S(1)} %fusion.12) | copy-start | bytes 11010052
  62.6 45.8 %copy-start.1 = (bf16[128,2048]{1,0:T(8,128)(2,1)S(1)}, bf16[128,2048]{1,0:T(8,128)(2,1)}, u32[]{:S(2)}) copy-start(bf16[128,2048]{1,0:T(8,128)(2,1)} %param.10) | copy-start | bytes 1572868
  75.2 34.3 %copy-start.3 = (f32[2048]{0:T(1024)S(1)}, f32[2048]{0:T(1024)}, u32[]{:S(2)}) copy-start(f32[2048]{0:T(1024)} %param.14) | copy-start | bytes 24580
  168.0 5.0 %copy-start.2 = (bf16[2,16,16,2176]{3,2,1,0:T(8,128)(2,1)S(1)}, bf16[2,16,16,2176]{3,2,1,0:T(8,128)(2,1)}, u32[]{:S(2)}) copy-start(bf16[2,16,16,2176]{3,2,1,0:T(8,128)(2,1)} %get-tuple-element.8) | copy-start | bytes 6684676
  173.0 14.6 %copy-start.4 = (f32[8,128]{1,0:T(8,128)S(1)}, f32[8,128]{1,0:T(8,128)}, u32[]{:S(2)}) copy-start(f32[8,128]{1,0:T(8,128)} %get-tuple-element.37) | copy-start | bytes 12292

commit v3 on v2

--- a/solution.py
+++ b/solution.py
@@ -7,6 +7,20 @@
 
 HOURS = 8
 MESH = pl.DeviceIdType.MESH
+
+
+def partner(e, k, n, sign=1):
+    if n & (n - 1):
+        return lax.rem(e + n + sign * k, n)
+    met, bit = 0, 1
+    while bit < n:
+        met = met + lax.rem(e // bit + k // bit, 2) * bit
+        bit *= 2
+    return met
+
+
+def outward(e, k, n, sign=1):
+    return lax.rem(e + n + sign * (n // 2 + (lax.rem(k, 2) * 2 - 1) * (k // 2)), n)
 
 
 def greet(n_expert, n_group):
@@ -59,7 +73,7 @@
     def start(self):
         @pl.loop(1, self.n_expert)
         def _(k):
-            self.across(lax.rem(self.e + k, self.n_expert), self.e).start()
+            self.across(partner(self.e, k, self.n_expert), self.e).start()
 
         self.own.start()
         for k in range(1, self.n_group):
@@ -68,7 +82,7 @@
     def forward(self, first, last):
         @pl.loop(first, last)
         def _(k):
-            row = lax.rem(self.e + self.n_expert - k, self.n_expert)
+            row = partner(self.e, k, self.n_expert, -1)
             self.across(row, row).wait_recv()
             for j in range(1, self.n_group):
                 self.over(self.out.at[self.d, row], row, j).start()
@@ -76,7 +90,7 @@
     def finish(self):
         @pl.loop(0, self.n_expert)
         def _(k):
-            row = lax.rem(self.e + self.n_expert - k, self.n_expert)
+            row = partner(self.e, k, self.n_expert, -1)
             for j in range(1, self.n_group):
                 self.over(self.out.at[self.d, row], row, j).wait_send()
                 came = lax.rem(self.d + self.n_group - j, self.n_group)
@@ -91,7 +105,7 @@
 
         @pl.loop(1, self.n_expert)
         def _(k):
-            self.across(lax.rem(self.e + k, self.n_expert), self.e).wait_send()
+            self.across(partner(self.e, k, self.n_expert), self.e).wait_send()
 
         self.own.wait()
 
@@ -159,15 +173,18 @@
             value = value + held[j - 1, row].astype(jnp.float32)
         return value.astype(out.dtype)
 
-    @pl.loop(1, n_expert + 1)
-    def _(k):
-        row = lax.rem(e + k, n_expert)
+    @pl.loop(1, n_expert)
+    def _(k):
+        row = outward(e, k, n_expert)
         for j in range(1, n_group):
             over(row, j).start()
 
+    for j in range(1, n_group):
+        over(e, j).start()
+
     @pl.loop(1, n_expert)
     def _(k):
-        row = lax.rem(e + k, n_expert)
+        row = outward(e, k, n_expert)
         summed[row] = total(row)
         across(row, e).start()
 
@@ -175,12 +192,12 @@
 
     @pl.loop(1, n_expert)
     def _(k):
-        row = lax.rem(e + n_expert - k, n_expert)
+        row = outward(e, k, n_expert, -1)
         across(row, row).wait_recv()
 
     @pl.loop(1, n_expert)
     def _(k):
-        across(lax.rem(e + k, n_expert), e).wait_send()
+        across(outward(e, k, n_expert), e).wait_send()
 
     @pl.loop(0, n_expert)
     def _(row):

time: 190 us -> 168 us (0.88); the launches traced: 189 us -> 165 us
  Pallas kernels: 126 us -> 102 us
    pallas_call x1, Pallas kernels: 51 us -> 37.6 us  [exchange(): pl.pallas_call(lambda *refs: exchange_kernel(n_expert, n_group, *refs), o...]
    pallas_call x1, Pallas kernels: 41.8 us -> 32 us  [dispatch(): pl.pallas_call(lambda *refs: dispatch_kernel(n_expert, n_group, *refs), o...]
where the time goes in v3:
time: 168 us; the launch traced here: 165 us
  Pallas kernels  102 us (61%)
  matrix products  52 us (31%)
  other arithmetic  6.78 us (4%)
  between operations  2.62 us (2%)
  local copies, waits for them, and re-layouts  2.07 us (1%)
    pallas_call x1, Pallas kernels, exchange(): pl.pallas_call(lambda *refs: exchange_kernel(n_expert, n_group, *refs), o...  37.6 us
    pallas_call x1, Pallas kernels, collect(): pl.pallas_call(lambda *refs: collect_kernel(n_expert, n_group, *refs), ou...  32 us
    pallas_call x1, Pallas kernels, dispatch(): pl.pallas_call(lambda *refs: dispatch_kernel(n_expert, n_group, *refs), o...  32 us
    dot_general x1, matrix products, local(): lax.dot_general(hidden, g_arrived, (((0,), (0,)), ((), ())), preferred_el...  14.6 us
    dot_general x1, matrix products, local(): jnp.dot(hidden, down_local, preferred_element_type=jnp.float32)  12.6 us
    dot_general x1, matrix products, local(): jnp.dot(arrived, up_local, preferred_element_type=jnp.float32)  12.6 us
    dot_general x1, matrix products, local(): lax.dot_general(g_loads, readout, (((1,), (1,)), ((), ())), preferred_ele...  4.4 us

profile of v3, /device:TPU:25, one launch (start us, length us, event | category | flops | bytes accessed | tf_op | source)
XLA Modules:
  0.0 165.0 jit_solution(15646506462935498751)
XLA Ops:
  0.6 0.0 copy-start
  0.6 0.7 fusion.49
  1.4 1.3 fusion.51
  2.7 0.7 multiply_reduce_fusion.4
  3.4 0.8 copy.42
  4.2 0.1 eq.65
  4.3 0.2 fusion.30
  4.5 0.1 reduce_sum.99
  4.7 0.1 copy.43
  4.8 0.7 multiply_add_fusion
  5.5 0.1 select_reduce_fusion
  5.6 2.5 %convolution_convert_fusion.2 = bf16[256,2048]{1,0:T(8,128)(2,1)} fusion(bf16[128,2048]{1,0:T(8,128)(2,1)} %param.10, f32[128,256]{1,0:T(8,128)S(1)} %get-tuple-element.15), kind=kOutput, calls=%fused_computation.23 | convolution fusion | flops 134774784 | bytes 1703936 | tf_op jit(solution)/shard_map/dot_general | solution.py:368
  8.1 32.0 %dispatch.1 = bf16[2,16,16,2048]{3,2,1,0:T(8,128)(2,1)} custom-call(bf16[16,16,2048]{2,1,0:T(8,128)(2,1)} %bitcast.43), custom_call_target="tpu_custom_call" | custom-call | tf_op jit(solution)/shard_map/dispatch/pallas_call | solution.py:133
  40.1 12.6 %fusion.12 = bf16[512,3584]{1,0:T(8,128)(2,1)S(1)} fusion(bf16[512,2048]{1,0:T(8,128)(2,1)} %bitcast.47, bf16[1,2048,3584]{2,1,0:T(8,128)(2,1)} %param.12), kind=kOutput, calls=%fused_computation.14 | convolution fusion | flops 7532707840 | bytes 20447232 | tf_op jit(solution)/shard_map/dot_general | solution.py:380
  52.7 0.0 copy-start.5
  52.7 0.0 copy-start.1
  52.7 12.6 %fusion.19 = bf16[512,2048]{1,0:T(8,128)(2,1)S(1)} fusion(bf16[512,3584]{1,0:T(8,128)(2,1)S(1)} %fusion.12, bf16[1,3584,2048]{2,1,0:T(8,128)(2,1)} %param.13), kind=kOutput, calls=%fused_computation.21 | convolution fusion | flops 7517241344 | bytes 20447232 | tf_op jit(solution)/shard_map/dot_general | solution.py:383
  65.4 0.0 copy-done.5
  65.4 0.0 copy-start.3
  65.4 32.0 %collect.1 = bf16[16,16,2048]{2,1,0:T(8,128)(2,1)S(1)} custom-call(bf16[2,16,16,2048]{3,2,1,0:T(8,128)(2,1)S(1)} %bitcast.41), custom_call_target="tpu_custom_call" | custom-call | tf_op jit(solution)/shard_map/collect/pallas_call | solution.py:210
  97.4 0.0 copy-done.1
  97.4 0.8 multiply_reduce_fusion
  98.2 0.1 multiply_reduce_fusion.2
  98.4 0.1 copy.44
  98.5 0.0 copy-done
  98.5 0.0 copy-done.3
  98.5 0.3 fusion.31
  98.9 0.5 convolution_convert_fusion.1
  99.3 1.1 fusion.28
  100.4 0.8 convolution_bitcast_fusion.refs_0_
  101.3 37.6 %exchange.1 = (f32[8,128]{1,0:T(8,128)}, f32[32,8,128]{2,1,0:T(8,128)}, bf16[2,16,16,2176]{3,2,1,0:T(8,128)(2,1)}) custom-call(f32[32,8,128]{2,1,0:T(8,128)} %convolution_bitcast_fusion.refs_0_, f32[32,8,128]{2,1,0:T(8,128)} %bitcast.48, bf16[16,16,2176]{2,1,0:T(8,128)(2,1)} %bitcast.42), custom_call_target="tpu_custom_call" | custom-call | tf_op jit(solution)/shard_map/exchange/pallas_call | solution.py:310
  138.8 1.5 multiply_reduce_fusion.1
  141.0 0.9 slice_convert_fusion
  142.0 0.3 fusion.38
  142.3 1.3 convolution_convert_fusion.3
  143.6 0.0 copy-start.2
  143.6 4.4 %fusion.15 = (f32[512]{0:T(512)S(1)}, f32[512,2048]{1,0:T(8,128)}) fusion(f32[2048]{0:T(1024)S(1)} %copy-done.3, bf16[512,2176]{1,0:T(8,128)(2,1)} %bitcast.45, bf16[512,128]{1,0:T(8,128)(2,1)S(1)} %convolution_convert_fusion.3, bf16[2048,128]{1,0:T(8,128)(2,1)S(1)} %copy-done), kind=kOutput, calls=%fused_computation.17 | convolution fusion | flops 272629248 | bytes 6957056 | tf_op jit(solution)/shard_map/dot_general | solution.py:427
  148.0 0.1 copy.45
  148.2 0.4 fusion.39
  148.6 0.0 copy-done.2
  148.6 0.0 copy-start.4
  148.6 14.6 %fusion.4 = bf16[1,3584,2048]{2,1,0:T(8,128)(2,1)} fusion(bf16[512,3584]{1,0:T(8,128)(2,1)} %copy-done.5, f32[512,2048]{1,0:T(8,128)} %get-tuple-element.31, f32[512]{0:T(512)S(1)} %get-tuple-element.10, f32[2048]{0:T(1024)S(1)} %copy-done.3, f32[512]{0:T(512)S(1)} %get-tuple-element.9, bf16[512,2176]{1,0:T(8,128)(2,1)S(1)} %bitcast.46), kind=kOutput, calls=%fused_computation.5 | convolution fusion | flops 7529824256 | bytes 24653824 | tf_op jit(solution)/shard_map/dot_general | solution.py:433
  163.2 0.0 copy-done.4
  163.2 0.6 copy.47
  (8 shorter events, 0.1 us)
Async XLA Ops:
  0.6 97.9 %copy-start = (bf16[2048,128]{1,0:T(8,128)(2,1)S(1)}, bf16[2048,128]{1,0:T(8,128)(2,1)}, u32[]{:S(2)}) copy-start(bf16[2048,128]{1,0:T(8,128)(2,1)} %param.15) | copy-start | bytes 1572868
  52.7 12.7 %copy-start.5 = (bf16[512,3584]{1,0:T(8,128)(2,1)}, bf16[512,3584]{1,0:T(8,128)(2,1)S(1)}, u32[]{:S(2)}) copy-start(bf16[512,3584]{1,0:T(8,128)(2,1)S(1)} %fusion.12) | copy-start | bytes 11010052
  52.7 44.7 %copy-start.1 = (bf16[128,2048]{1,0:T(8,128)(2,1)S(1)}, bf16[128,2048]{1,0:T(8,128)(2,1)}, u32[]{:S(2)}) copy-start(bf16[128,2048]{1,0:T(8,128)(2,1)} %param.10) | copy-start | bytes 1572868
  65.4 33.1 %copy-start.3 = (f32[2048]{0:T(1024)S(1)}, f32[2048]{0:T(1024)}, u32[]{:S(2)}) copy-start(f32[2048]{0:T(1024)} %param.14) | copy-start | bytes 24580
  143.6 5.0 %copy-start.2 = (bf16[2,16,16,2176]{3,2,1,0:T(8,128)(2,1)S(1)}, bf16[2,16,16,2176]{3,2,1,0:T(8,128)(2,1)}, u32[]{:S(2)}) copy-start(bf16[2,16,16,2176]{3,2,1,0:T(8,128)(2,1)} %get-tuple-element.8) | copy-start | bytes 6684676
  148.6 14.6 %copy-start.4 = (f32[8,128]{1,0:T(8,128)S(1)}, f32[8,128]{1,0:T(8,128)}, u32[]{:S(2)}) copy-start(f32[8,128]{1,0:T(8,128)} %get-tuple-element.37) | copy-start | bytes 12292
